TPU v7x, 512 devices: a whole 4x8x8 slice. The times are simulated.
512 devices in a mesh: member: 8 (over y_lo, core), space: 64 (over z, x, y_hi).
Axes of the slice: x: 4, y: 8 (y_hi: 2, y_lo: 4; y = y_hi * 4 + y_lo), z: 8, core: 2. Of those that a mesh axis runs over, the one named last changes fastest.
Arguments:
- latent: bfloat16 [8, 8192, 1024], P('member', 'space'), may hold values from -6 to 6
- w_query: bfloat16 [1024, 512], replicated, may hold values from -0.1875 to 0.1875
- w_key: bfloat16 [1024, 512], replicated, may hold values from -0.1875 to 0.1875
- w_value: bfloat16 [1024, 512], replicated, may hold values from -0.1875 to 0.1875
- w_out: bfloat16 [512, 1024], replicated, may hold values from -0.25 to 0.25
- w_decode: bfloat16 [100, 1024], replicated, may hold values from -0.1875 to 0.1875
- window: int32 [8192, 32], P('space'), may hold values from 0 to 8191, as said below
- decoder_src: int32 [32768, 3], P('space'), may hold values from 0 to 8191, as said below
- edge_weight: float32 [32768, 3], P('space'), may hold values from 0.3 to 1
- target: bfloat16 [100, 32768], P(None, 'space'), may hold values from -6 to 6
- area: float32 [32768], P('space'), may hold values from 0.5 to 2
Outputs:
- latent_grad: bfloat16 [8, 8192, 1024], P('member', 'space')
Inputs may be any that keep to these rules, and one draw needn't show every extreme that they name: `window`: every entry of row i lies within 64 of i; every row lists i - 64 and i + 64 where these rows exist, the other entries are clipped to the grid. `decoder_src`: for grid point g the entries lie within 64 of the centre (g // 512) * 128 + ((g % 512) * 128) // 512; each point lists centre - 64 and centre + 64 where these rows exist, clipped to the grid.
All inputs are finite; a program needn't handle non-finite values.
Results may differ from a plain program's by a relative error of at most 0.04.
Values may be sent and summed in bfloat16 or wider, within the bound.
A program may use at most 64 MiB of HBM per device.

v0:
```python
import jax
import jax.numpy as jnp
from jax import lax
from jax.sharding import PartitionSpec as P

HEADS = 8
DH = 64
R = 64
KD = 3


score_scale = 6.0
eps_norm = 1e-06
delta_smooth = 0.1


def with_halo(block, sides, width):
    for axis, dim in sides:
        count = lax.axis_size(axis)
        forward = [(i, i + 1) for i in range(count - 1)]
        backward = [(target, source) for source, target in forward]
        low = lax.ppermute(
            lax.slice_in_dim(block, block.shape[dim] - width, None, axis=dim), axis, forward
        )
        high = lax.ppermute(lax.slice_in_dim(block, 0, width, axis=dim), axis, backward)
        block = jnp.concatenate([low, block, high], axis=dim)
    return block


def normalize_heads(projected):
    grouped = projected.reshape(projected.shape[0], HEADS, DH)
    factor = lax.rsqrt(jnp.mean(grouped * grouped, axis=2, keepdims=True) + eps_norm)
    return (grouped * factor, factor)


def norm_backward(grad_hat, unit_rows, factor):
    return factor * (grad_hat - unit_rows * jnp.mean(grad_hat * unit_rows, axis=2, keepdims=True))


def smooth_slope(difference):
    return difference * lax.rsqrt(difference * difference + delta_smooth * delta_smooth)


def attend(key_rows, query_rows, local_index, w_query, w_key, w_value, w_out):
    count_query = query_rows.shape[0]
    count_key = key_rows.shape[0]
    queries = jnp.dot(query_rows, w_query, preferred_element_type=jnp.float32)
    key_proj = jnp.dot(key_rows, w_key, preferred_element_type=jnp.float32)
    value_low = (
        jnp.dot(key_rows, w_value, preferred_element_type=jnp.float32)
        .astype(jnp.bfloat16)
        .reshape(count_key, HEADS, DH)
    )
    query_hat, query_factor = normalize_heads(queries)
    key_hat, key_factor = normalize_heads(key_proj)
    query_low = query_hat.astype(jnp.bfloat16)
    key_low = key_hat.astype(jnp.bfloat16)
    safe_index = jnp.clip(local_index, 0, count_key - 1)
    row_number = jnp.arange(count_query, dtype=jnp.int32)[:, None]
    counts = jnp.zeros((count_query, count_key), jnp.float32).at[row_number, safe_index].add(1.0)
    scores = jnp.einsum("qhd,khd->hqk", query_low, key_low, preferred_element_type=jnp.float32) * (
        score_scale / DH
    )
    weighted = counts[None] * jnp.exp(scores)
    probs = weighted / jnp.sum(weighted, axis=2, keepdims=True)
    probs_low = probs.astype(jnp.bfloat16)
    mixed = jnp.einsum(
        "hqk,khd->qhd", probs_low, value_low, preferred_element_type=jnp.float32
    ).astype(jnp.bfloat16)
    projected = jnp.dot(
        mixed.reshape(count_query, HEADS * DH), w_out, preferred_element_type=jnp.float32
    )
    output = (query_rows.astype(jnp.float32) + projected).astype(jnp.bfloat16)
    saved = (
        query_hat,
        query_factor,
        query_low,
        key_hat,
        key_factor,
        key_low,
        value_low,
        probs,
        probs_low,
    )
    return (output, saved)


def per_device(
    latent, w_query, w_key, w_value, w_out, w_decode, window, decoder_src, edge_weight, target, area
):
    hidden = latent[0]
    count_own = hidden.shape[0]
    width = hidden.shape[1]
    points = target.shape[1]
    members = lax.axis_size("member") * latent.shape[0]
    anchor = lax.axis_index("space") * count_own - R
    near_rows = with_halo(hidden, (("space", 0),), R)
    output, saved = attend(near_rows, hidden, window - anchor, w_query, w_key, w_value, w_out)
    output_ext = with_halo(output, (("space", 0),), R)
    (
        query_hat,
        query_factor,
        query_low,
        key_hat,
        key_factor,
        key_low,
        value_low,
        probs,
        probs_low,
    ) = saved
    source = decoder_src - anchor
    gathered_sum = jnp.zeros((points, width), jnp.float32)
    for slot in range(KD):
        gathered_sum = gathered_sum + edge_weight[:, slot, None] * output_ext[
            source[:, slot]
        ].astype(jnp.float32)
    aggregate = gathered_sum.astype(jnp.bfloat16)
    prediction = jnp.einsum(
        "vc,gc->vg", w_decode, aggregate, preferred_element_type=jnp.float32
    ).astype(jnp.bfloat16)
    truth = target.astype(jnp.float32)
    own_value = prediction.astype(jnp.float32)
    slope_sum = jnp.sum(
        smooth_slope(
            own_value[None]
            - lax.all_gather(prediction[None], "member", axis=0, tiled=True).astype(jnp.float32)
        ),
        axis=0,
    )
    dpred = (area[None, :] * (smooth_slope(own_value - truth) - slope_sum / (members - 1))).astype(
        jnp.bfloat16
    )
    dagg = jnp.einsum("vg,vc->gc", dpred, w_decode, preferred_element_type=jnp.float32)
    dout_ext = jnp.zeros((count_own + 2 * R, width), jnp.float32)
    for slot in range(KD):
        dout_ext = dout_ext.at[source[:, slot]].add(edge_weight[:, slot, None] * dagg)
    edge_rows = jnp.concatenate([dout_ext[:R], dout_ext[R + count_own :]], axis=0)
    beside_all = with_halo(edge_rows.astype(jnp.bfloat16), (("space", 0),), R).astype(
        edge_rows.dtype
    )
    dout = (
        dout_ext[R : R + count_own]
        .at[:R]
        .add(beside_all[:R])
        .at[count_own - R :]
        .add(beside_all[3 * R :])
    )
    dout_low = dout.astype(jnp.bfloat16)
    dmixed = jnp.einsum("qc,ec->qe", dout_low, w_out, preferred_element_type=jnp.float32).astype(
        jnp.bfloat16
    )
    dmixed = dmixed.reshape(count_own, HEADS, DH)
    dprob = jnp.einsum("qhd,khd->hqk", dmixed, value_low, preferred_element_type=jnp.float32)
    row_term = jnp.sum(probs * dprob, axis=2, keepdims=True)
    dscore = (probs * (dprob - row_term)).astype(jnp.bfloat16)
    dq_hat = jnp.einsum("hqk,khd->qhd", dscore, key_low, preferred_element_type=jnp.float32) * (
        score_scale / DH
    )
    dk_hat = jnp.einsum("hqk,qhd->khd", dscore, query_low, preferred_element_type=jnp.float32) * (
        score_scale / DH
    )
    dvalue = jnp.einsum("hqk,qhd->khd", probs_low, dmixed, preferred_element_type=jnp.float32)
    span = count_own + 2 * R
    key_parts = jnp.concatenate(
        [dk_hat.reshape(span, HEADS * DH), dvalue.reshape(span, HEADS * DH)], axis=1
    )
    key_edges = jnp.concatenate([key_parts[:R], key_parts[R + count_own :]], axis=0)
    key_around = with_halo(key_edges.astype(jnp.bfloat16), (("space", 0),), R).astype(
        key_edges.dtype
    )
    total = (
        key_parts[R : R + count_own]
        .at[:R]
        .add(key_around[:R])
        .at[count_own - R :]
        .add(key_around[3 * R :])
    )
    dk_total = total[:, : HEADS * DH].reshape(count_own, HEADS, DH)
    dq_low = (
        norm_backward(dq_hat, query_hat, query_factor)
        .reshape(count_own, HEADS * DH)
        .astype(jnp.bfloat16)
    )
    dk_low = (
        norm_backward(dk_total, key_hat[R : R + count_own], key_factor[R : R + count_own])
        .reshape(count_own, HEADS * DH)
        .astype(jnp.bfloat16)
    )
    dvalue_low = total[:, HEADS * DH :].astype(jnp.bfloat16)
    grad = dout + jnp.einsum("qe,ce->qc", dq_low, w_query, preferred_element_type=jnp.float32)
    grad = grad + jnp.einsum("qe,ce->qc", dk_low, w_key, preferred_element_type=jnp.float32)
    grad = grad + jnp.einsum("qe,ce->qc", dvalue_low, w_value, preferred_element_type=jnp.float32)
    return grad.astype(jnp.bfloat16)[None]


def solution(mesh):
    in_specs = (
        P("member", "space", None),
        P(),
        P(),
        P(),
        P(),
        P(),
        P("space", None),
        P("space", None),
        P("space", None),
        P(None, "space"),
        P("space"),
    )
    out_specs = P("member", "space", None)
    return jax.shard_map(
        per_device, mesh=mesh, in_specs=in_specs, out_specs=out_specs, check_vma=False
    )
```

profile of v0, /device:TPU:252, one launch (start us, length us, event | category | flops | bytes accessed | tf_op | source)
XLA Modules:
  0.0 203.0 jit_solution(651097297202947818)
XLA Ops:
  1.1 5.3 %collective-permute-start = (bf16[64,1024]{1,0:T(8,128)(2,1)S(1)}, bf16[64,1024]{1,0:T(8,128)(2,1)S(1)}, u32[]{:S(2)}, u32[]{:S(2)}) collective-permute-start(bf16[64,1024]{1,0:T(8,128)(2,1)S(1)} %get-tuple-element.59), channel_id=1, source_target_pairs={{0,1},{1,2},{2,3},{3,4},{4,5},{5,6},{6,7},{7,8},{8,9},{9,10},{10,1... | collective-permute-start | bytes 393224 | tf_op jit(solution)/shard_map/ppermute | solution.py:22
  6.5 4.4 %collective-permute-start.1 = (bf16[64,1024]{1,0:T(8,128)(2,1)S(1)}, bf16[64,1024]{1,0:T(8,128)(2,1)S(1)}, u32[]{:S(2)}, u32[]{:S(2)}) collective-permute-start(bf16[64,1024]{1,0:T(8,128)(2,1)S(1)} %get-tuple-element.60), channel_id=1, source_target_pairs={{1,0},{2,1},{3,2},{4,3},{5,4},{6,5},{7,6},{8,7},{9,8},{10,9},{11,1... | collective-permute-start | bytes 393224 | tf_op jit(solution)/shard_map/ppermute | solution.py:25
  16.8 28.8 %scatter_custom_fusion.3 = f32[32768]{0:T(1024)S(1)} fusion(s32[4096]{0:T(1024)S(1)} %reshape.229, f32[4096]{0:T(1024)S(1)} %broadcast.135, f32[]{:T(128)} %constant.128.clone.1), kind=kCustom, calls=%fused_computation.91 | custom fusion | flops 4096 | bytes 131076
  53.4 6.2 %collective-permute-start.2 = (bf16[64,1024]{1,0:T(8,128)(2,1)S(1)}, bf16[64,1024]{1,0:T(8,128)(2,1)S(1)}, u32[]{:S(2)}, u32[]{:S(2)}) collective-permute-start(bf16[64,1024]{1,0:T(8,128)(2,1)S(1)} %get-tuple-element.57), channel_id=1, source_target_pairs={{0,1},{1,2},{2,3},{3,4},{4,5},{5,6},{6,7},{7,8},{8,9},{9,10},{10,1... | collective-permute-start | bytes 393224 | tf_op jit(solution)/shard_map/ppermute | solution.py:22
  59.7 3.5 %collective-permute-start.3 = (bf16[64,1024]{1,0:T(8,128)(2,1)S(1)}, bf16[64,1024]{1,0:T(8,128)(2,1)S(1)}, u32[]{:S(2)}, u32[]{:S(2)}) collective-permute-start(bf16[64,1024]{1,0:T(8,128)(2,1)S(1)} %get-tuple-element.58), channel_id=1, source_target_pairs={{1,0},{2,1},{3,2},{4,3},{5,4},{6,5},{7,6},{8,7},{9,8},{10,9},{11,1... | collective-permute-start | bytes 393224 | tf_op jit(solution)/shard_map/ppermute | solution.py:25
  63.2 3.0 %collective-permute-done.2 = bf16[64,1024]{1,0:T(8,128)(2,1)S(1)} collective-permute-done((bf16[64,1024]{1,0:T(8,128)(2,1)S(1)}, bf16[64,1024]{1,0:T(8,128)(2,1)S(1)}, u32[]{:S(2)}, u32[]{:S(2)}) %collective-permute-start.2) | collective-permute-done | bytes 131104 | tf_op jit(solution)/shard_map/ppermute | solution.py:22
  66.3 8.2 %collective-permute-done.3 = bf16[64,1024]{1,0:T(8,128)(2,1)S(1)} collective-permute-done((bf16[64,1024]{1,0:T(8,128)(2,1)S(1)}, bf16[64,1024]{1,0:T(8,128)(2,1)S(1)}, u32[]{:S(2)}, u32[]{:S(2)}) %collective-permute-start.3) | collective-permute-done | bytes 131104 | tf_op jit(solution)/shard_map/ppermute | solution.py:25
  76.6 2.8 %gather_fusion.1 = bf16[512,1024]{1,0:T(8,128)(2,1)} fusion(bf16[256,1024]{1,0:T(8,128)(2,1)S(1)} %pad_maximum_fusion.2, s32[1024]{0:T(1024)S(1)} %pad_clamp_fusion.1), kind=kCustom, calls=%fused_computation.1 | custom fusion | bytes 2099200 | tf_op jit(solution)/shard_map/gather | solution.py:114
  79.3 2.8 %gather_fusion = bf16[512,1024]{1,0:T(8,128)(2,1)} fusion(bf16[256,1024]{1,0:T(8,128)(2,1)S(1)} %pad_maximum_fusion.2, s32[1024]{0:T(1024)S(1)} %pad_clamp_fusion.2), kind=kCustom, calls=%fused_computation | custom fusion | bytes 2099200 | tf_op jit(solution)/shard_map/gather | solution.py:114
  82.1 2.4 %bitcast_convert_fusion = (f32[100,512]{1,0:T(8,128)S(1)}, bf16[512,100]{0,1:T(8,128)(2,1)S(1)}) fusion(bf16[100,1024]{1,0:T(8,128)(2,1)S(1)} %copy-done.12, bf16[512,1024]{1,0:T(8,128)(2,1)S(1)} %gather_fusion.2, bf16[512,1024]{1,0:T(8,128)(2,1)} %gather_fusion.1, bf16[512,1024]{1,0:T(8,128)(2,1)} %gather_fusion, f32[512]{0:T(512)S(1)} %bitcast.98, ...), kind=kOutput, calls=%fused_computation.87 | convolution fusion | flops 109678592 | bytes 3663872 | tf_op jit(solution)/shard_map/vc,gc->vg/dot_general | solution.py:118
  84.6 16.3 %all-gather.1 = bf16[8,100,512]{2,1,0:T(8,128)(2,1)S(1)} all-gather(bf16[1,100,512]{2,1,0:T(8,128)(2,1)S(1)} %bitcast.88), channel_id=2, replica_groups=mesh['member'=8,'space'=64] {'member'}, dimensions={0}, use_global_device_ids=true | all-gather | bytes 921600 | tf_op jit(solution)/shard_map/all_gather | solution.py:126
  101.8 6.0 %scatter_custom_fusion = f32[256,1024]{1,0:T(8,128)} fusion(s32[512]{0:T(512)} %bitcast.97, f32[512,1024]{1,0:T(8,128)S(1)} %fusion.38, f32[512]{0:T(512)S(1)} %bitcast.91, f32[]{:T(128)} %constant.128.clone.1), kind=kCustom, calls=%fused_computation.11 | custom fusion | flops 1048576 | bytes 3148288 | tf_op jit(solution)/shard_map/scatter-add | solution.py:136
  107.9 7.2 %scatter_custom_fusion.1 = f32[256,1024]{1,0:T(8,128)} fusion(f32[256,1024]{1,0:T(8,128)} %scatter_custom_fusion, s32[512]{0:T(512)} %bitcast.95, f32[512,1024]{1,0:T(8,128)S(1)} %fusion.38, f32[512]{0:T(512)} %bitcast.101), kind=kCustom, calls=%fused_computation.9 | custom fusion | flops 1048576 | bytes 3147776 | tf_op jit(solution)/shard_map/scatter-add | solution.py:136
  115.1 7.2 %scatter_custom_fusion.2 = f32[256,1024]{1,0:T(8,128)} fusion(f32[256,1024]{1,0:T(8,128)} %scatter_custom_fusion.1, s32[512]{0:T(512)} %bitcast.93, f32[512,1024]{1,0:T(8,128)S(1)} %fusion.38, f32[512]{0:T(512)S(1)} %bitcast.99), kind=kCustom, calls=%fused_computation.7 | custom fusion | flops 1048576 | bytes 3147776 | tf_op jit(solution)/shard_map/scatter-add | solution.py:136
  123.7 8.5 %collective-permute-start.4 = (bf16[64,1024]{1,0:T(8,128)(2,1)S(1)}, bf16[64,1024]{1,0:T(8,128)(2,1)S(1)}, u32[]{:S(2)}, u32[]{:S(2)}) collective-permute-start(bf16[64,1024]{1,0:T(8,128)(2,1)S(1)} %get-tuple-element.55), channel_id=1, source_target_pairs={{0,1},{1,2},{2,3},{3,4},{4,5},{5,6},{6,7},{7,8},{8,9},{9,10},{10,1... | collective-permute-start | bytes 393224 | tf_op jit(solution)/shard_map/ppermute | solution.py:22
  134.2 5.0 %collective-permute-done.4 = bf16[64,1024]{1,0:T(8,128)(2,1)S(1)} collective-permute-done((bf16[64,1024]{1,0:T(8,128)(2,1)S(1)}, bf16[64,1024]{1,0:T(8,128)(2,1)S(1)}, u32[]{:S(2)}, u32[]{:S(2)}) %collective-permute-start.4) | collective-permute-done | bytes 131104 | tf_op jit(solution)/shard_map/ppermute | solution.py:22
  139.2 10.1 %collective-permute-done.5 = bf16[64,1024]{1,0:T(8,128)(2,1)S(1)} collective-permute-done((bf16[64,1024]{1,0:T(8,128)(2,1)S(1)}, bf16[64,1024]{1,0:T(8,128)(2,1)S(1)}, u32[]{:S(2)}, u32[]{:S(2)}) %collective-permute-start.5) | collective-permute-done | bytes 131104 | tf_op jit(solution)/shard_map/ppermute | solution.py:25
  153.4 2.8 %multiply_reduce_fusion = (f32[8,128]{1,0:T(8,128)S(1)}, f32[8,128,256]{2,1,0:T(8,128)}) fusion(f32[8,128,256]{2,1,0:T(8,128)} %fusion.60, f32[128,256]{1,0:T(8,128)S(1)} %reshape.180, f32[256,8,64]{0,2,1:T(8,128)S(1)} %copy-done.2, f32[128,8,64]{0,2,1:T(8,128)S(1)} %get-tuple-element.70, f32[128,8]{0,1:T(8,128)S(1)} %add_rsqrt_fusion.1), kind=kOutput, calls=%fused_computation.44 | convolution fusion | flops 35127552 | bytes 3022848 | tf_op jit(solution)/shard_map/div | solution.py:65
  158.8 5.6 %collective-permute-start.6 = (bf16[64,1024]{0,1:T(8,128)(2,1)S(1)}, bf16[64,1024]{0,1:T(8,128)(2,1)S(1)}, u32[]{:S(2)}, u32[]{:S(2)}) collective-permute-start(bf16[64,1024]{0,1:T(8,128)(2,1)S(1)} %get-tuple-element.53), channel_id=1, source_target_pairs={{0,1},{1,2},{2,3},{3,4},{4,5},{5,6},{6,7},{7,8},{8,9},{9,10},{10,1... | collective-permute-start | bytes 393224 | tf_op jit(solution)/shard_map/ppermute | solution.py:22
  164.5 4.1 %collective-permute-start.7 = (bf16[64,1024]{0,1:T(8,128)(2,1)S(1)}, bf16[64,1024]{0,1:T(8,128)(2,1)S(1)}, u32[]{:S(2)}, u32[]{:S(2)}) collective-permute-start(bf16[64,1024]{0,1:T(8,128)(2,1)S(1)} %get-tuple-element.54), channel_id=1, source_target_pairs={{1,0},{2,1},{3,2},{4,3},{5,4},{6,5},{7,6},{8,7},{9,8},{10,9},{11,1... | collective-permute-start | bytes 393224 | tf_op jit(solution)/shard_map/ppermute | solution.py:25
  169.3 10.3 %collective-permute-done.6 = bf16[64,1024]{0,1:T(8,128)(2,1)S(1)} collective-permute-done((bf16[64,1024]{0,1:T(8,128)(2,1)S(1)}, bf16[64,1024]{0,1:T(8,128)(2,1)S(1)}, u32[]{:S(2)}, u32[]{:S(2)}) %collective-permute-start.6) | collective-permute-done | bytes 131104 | tf_op jit(solution)/shard_map/ppermute | solution.py:22
  179.6 10.4 %collective-permute-done.7 = bf16[64,1024]{0,1:T(8,128)(2,1)S(1)} collective-permute-done((bf16[64,1024]{0,1:T(8,128)(2,1)S(1)}, bf16[64,1024]{0,1:T(8,128)(2,1)S(1)}, u32[]{:S(2)}, u32[]{:S(2)}) %collective-permute-start.7) | collective-permute-done | bytes 131104 | tf_op jit(solution)/shard_map/ppermute | solution.py:25
  192.3 3.8 %scatter-add.54 = f32[128,1024]{0,1:T(8,128)S(1)} dynamic-update-slice(f32[128,1024]{0,1:T(8,128)S(1)} %fusion.21, f32[64,1024]{0,1:T(8,128)} %fusion.23, s32[]{:T(128)} %constant.132.clone.1, s32[]{:T(128)} %constant.132.clone.1) | dynamic-update-slice | bytes 524292 | tf_op jit(solution)/shard_map/scatter-add | solution.py:174
  197.5 3.1 %scatter-add.55 = f32[128,1024]{0,1:T(8,128)S(1)} dynamic-update-slice(f32[128,1024]{0,1:T(8,128)S(1)} %scatter-add.54, f32[64,1024]{0,1:T(8,128)S(1)} %slice_add_fusion, s32[]{:T(128)} %constant.141.clone.1, s32[]{:T(128)} %constant.132.clone.1) | dynamic-update-slice | bytes 524292 | tf_op jit(solution)/shard_map/scatter-add | solution.py:176
  (110 shorter events, 34.4 us)
Async XLA Ops:
  0.0 48.3 %copy-start = (bf16[1024,512]{1,0:T(8,128)(2,1)S(1)}, bf16[1024,512]{1,0:T(8,128)(2,1)}, u32[]{:S(2)}) copy-start(bf16[1024,512]{1,0:T(8,128)(2,1)} %param.21) | copy-start | bytes 3145732
  0.0 16.1 %copy-start.8 = (bf16[1,128,1024]{2,1,0:T(8,128)(2,1)S(1)}, bf16[1,128,1024]{2,1,0:T(8,128)(2,1)}, u32[]{:S(2)}) copy-start(bf16[1,128,1024]{2,1,0:T(8,128)(2,1)} %param.19) | copy-start | bytes 786436
  1.1 44.6 %collective-permute-start = (bf16[64,1024]{1,0:T(8,128)(2,1)S(1)}, bf16[64,1024]{1,0:T(8,128)(2,1)S(1)}, u32[]{:S(2)}, u32[]{:S(2)}) collective-permute-start(bf16[64,1024]{1,0:T(8,128)(2,1)S(1)} %get-tuple-element.59), channel_id=1, source_target_pairs={{0,1},{1,2},{2,3},{3,4},{4,5},{5,6},{6,7},{7,8},{8,9},{9,10},{10,1... | collective-permute-start | bytes 393224 | tf_op jit(solution)/shard_map/ppermute | solution.py:22
  6.5 39.2 %collective-permute-start.1 = (bf16[64,1024]{1,0:T(8,128)(2,1)S(1)}, bf16[64,1024]{1,0:T(8,128)(2,1)S(1)}, u32[]{:S(2)}, u32[]{:S(2)}) collective-permute-start(bf16[64,1024]{1,0:T(8,128)(2,1)S(1)} %get-tuple-element.60), channel_id=1, source_target_pairs={{1,0},{2,1},{3,2},{4,3},{5,4},{6,5},{7,6},{8,7},{9,8},{10,9},{11,1... | collective-permute-start | bytes 393224 | tf_op jit(solution)/shard_map/ppermute | solution.py:25
  11.7 70.5 %copy-start.18 = (f32[512,1]{0,1:T(1,128)}, f32[512,1]{0,1:T(1,128)S(1)}, u32[]{:S(2)}) copy-start(f32[512,1]{0,1:T(1,128)S(1)} %get-tuple-element.62) | copy-start | bytes 6148
  11.7 70.5 %copy-start.20 = (f32[512,1]{0,1:T(1,128)}, f32[512,1]{0,1:T(1,128)S(1)}, u32[]{:S(2)}) copy-start(f32[512,1]{0,1:T(1,128)S(1)} %get-tuple-element.63) | copy-start | bytes 6148
  12.4 33.2 %copy-start.15 = (s32[512,1]{0,1:T(1,128)}, s32[512,1]{0,1:T(1,128)S(1)}, u32[]{:S(2)}) copy-start(s32[512,1]{0,1:T(1,128)S(1)} %get-tuple-element.65) | copy-start | bytes 6148
  12.4 50.8 %copy-start.16 = (s32[512,1]{0,1:T(1,128)}, s32[512,1]{0,1:T(1,128)S(1)}, u32[]{:S(2)}) copy-start(s32[512,1]{0,1:T(1,128)S(1)} %get-tuple-element.64) | copy-start | bytes 6148
  12.4 50.8 %copy-start.17 = (s32[512,1]{0,1:T(1,128)}, s32[512,1]{0,1:T(1,128)S(1)}, u32[]{:S(2)}) copy-start(s32[512,1]{0,1:T(1,128)S(1)} %get-tuple-element.66) | copy-start | bytes 6148
  53.4 12.8 %collective-permute-start.2 = (bf16[64,1024]{1,0:T(8,128)(2,1)S(1)}, bf16[64,1024]{1,0:T(8,128)(2,1)S(1)}, u32[]{:S(2)}, u32[]{:S(2)}) collective-permute-start(bf16[64,1024]{1,0:T(8,128)(2,1)S(1)} %get-tuple-element.57), channel_id=1, source_target_pairs={{0,1},{1,2},{2,3},{3,4},{4,5},{5,6},{6,7},{7,8},{8,9},{9,10},{10,1... | collective-permute-start | bytes 393224 | tf_op jit(solution)/shard_map/ppermute | solution.py:22
  59.7 14.8 %collective-permute-start.3 = (bf16[64,1024]{1,0:T(8,128)(2,1)S(1)}, bf16[64,1024]{1,0:T(8,128)(2,1)S(1)}, u32[]{:S(2)}, u32[]{:S(2)}) collective-permute-start(bf16[64,1024]{1,0:T(8,128)(2,1)S(1)} %get-tuple-element.58), channel_id=1, source_target_pairs={{1,0},{2,1},{3,2},{4,3},{5,4},{6,5},{7,6},{8,7},{9,8},{10,9},{11,1... | collective-permute-start | bytes 393224 | tf_op jit(solution)/shard_map/ppermute | solution.py:25
  79.3 2.8 %copy-start.12 = (bf16[100,1024]{1,0:T(8,128)(2,1)S(1)}, bf16[100,1024]{1,0:T(8,128)(2,1)}, u32[]{:S(2)}) copy-start(bf16[100,1024]{1,0:T(8,128)(2,1)} %param.24) | copy-start | bytes 614404
  84.5 16.8 %copy-start.13 = (bf16[100,1024]{1,0:T(8,128)(2,1)S(1)}, bf16[100,1024]{1,0:T(8,128)(2,1)}, u32[]{:S(2)}) copy-start(bf16[100,1024]{1,0:T(8,128)(2,1)} %param.24) | copy-start | bytes 614404
  84.5 16.8 %copy-start.14 = (bf16[100,512]{1,0:T(8,128)(2,1)S(1)}, bf16[100,512]{1,0:T(8,128)(2,1)}, u32[]{:S(2)}) copy-start(bf16[100,512]{1,0:T(8,128)(2,1)} %param.28) | copy-start | bytes 307204
  84.6 16.8 %copy-start.21 = (f32[512]{0:T(512)S(1)}, f32[512]{0:T(512)}, u32[]{:S(2)}) copy-start(f32[512]{0:T(512)} %param.29) | copy-start | bytes 6148
  107.9 7.2 %copy-start.19 = (f32[512,1]{0,1:T(1,128)S(1)}, f32[512,1]{0,1:T(1,128)}, u32[]{:S(2)}) copy-start(f32[512,1]{0,1:T(1,128)} %copy-done.18) | copy-start | bytes 6148
  122.2 12.0 %copy-start.3 = (f32[256,1024]{1,0:T(8,128)S(1)}, f32[256,1024]{1,0:T(8,128)}, u32[]{:S(2)}) copy-start(f32[256,1024]{1,0:T(8,128)} %scatter_custom_fusion.2) | copy-start | bytes 3145732
  123.6 25.8 %copy-start.7 = (bf16[512,1024]{1,0:T(8,128)(2,1)S(1)}, bf16[512,1024]{1,0:T(8,128)(2,1)}, u32[]{:S(2)}) copy-start(bf16[512,1024]{1,0:T(8,128)(2,1)} %param.23) | copy-start | bytes 3145732
  123.7 15.6 %collective-permute-start.4 = (bf16[64,1024]{1,0:T(8,128)(2,1)S(1)}, bf16[64,1024]{1,0:T(8,128)(2,1)S(1)}, u32[]{:S(2)}, u32[]{:S(2)}) collective-permute-start(bf16[64,1024]{1,0:T(8,128)(2,1)S(1)} %get-tuple-element.55), channel_id=1, source_target_pairs={{0,1},{1,2},{2,3},{3,4},{4,5},{5,6},{6,7},{7,8},{8,9},{9,10},{10,1... | collective-permute-start | bytes 393224 | tf_op jit(solution)/shard_map/ppermute | solution.py:22
  132.2 17.2 %collective-permute-start.5 = (bf16[64,1024]{1,0:T(8,128)(2,1)S(1)}, bf16[64,1024]{1,0:T(8,128)(2,1)S(1)}, u32[]{:S(2)}, u32[]{:S(2)}) collective-permute-start(bf16[64,1024]{1,0:T(8,128)(2,1)S(1)} %get-tuple-element.56), channel_id=1, source_target_pairs={{1,0},{2,1},{3,2},{4,3},{5,4},{6,5},{7,6},{8,7},{9,8},{10,9},{11,1... | collective-permute-start | bytes 393224 | tf_op jit(solution)/shard_map/ppermute | solution.py:25
  150.1 3.3 %copy-start.2 = (f32[256,8,64]{0,2,1:T(8,128)S(1)}, f32[256,8,64]{0,2,1:T(8,128)}, u32[]{:S(2)}) copy-start(f32[256,8,64]{0,2,1:T(8,128)} %copy-done.1) | copy-start | bytes 1572868
  158.3 10.3 %copy-start.4 = (bf16[1024,512]{1,0:T(8,128)(2,1)S(1)}, bf16[1024,512]{1,0:T(8,128)(2,1)}, u32[]{:S(2)}) copy-start(bf16[1024,512]{1,0:T(8,128)(2,1)} %param.20) | copy-start | bytes 3145732
  158.8 20.8 %collective-permute-start.6 = (bf16[64,1024]{0,1:T(8,128)(2,1)S(1)}, bf16[64,1024]{0,1:T(8,128)(2,1)S(1)}, u32[]{:S(2)}, u32[]{:S(2)}) collective-permute-start(bf16[64,1024]{0,1:T(8,128)(2,1)S(1)} %get-tuple-element.53), channel_id=1, source_target_pairs={{0,1},{1,2},{2,3},{3,4},{4,5},{5,6},{6,7},{7,8},{8,9},{9,10},{10,1... | collective-permute-start | bytes 393224 | tf_op jit(solution)/shard_map/ppermute | solution.py:22
  164.5 25.5 %collective-permute-start.7 = (bf16[64,1024]{0,1:T(8,128)(2,1)S(1)}, bf16[64,1024]{0,1:T(8,128)(2,1)S(1)}, u32[]{:S(2)}, u32[]{:S(2)}) collective-permute-start(bf16[64,1024]{0,1:T(8,128)(2,1)S(1)} %get-tuple-element.54), channel_id=1, source_target_pairs={{1,0},{2,1},{3,2},{4,3},{5,4},{6,5},{7,6},{8,7},{9,8},{10,9},{11,1... | collective-permute-start | bytes 393224 | tf_op jit(solution)/shard_map/ppermute | solution.py:25
  (8 other events, 12.5 us)
where the time goes:
time: 204 us; the launch traced here: 203 us
  other arithmetic  59.1 us (29%)
  waiting for transfers between devices  46.9 us (23%)
  starting transfers between devices  39.7 us (19%)
  local copies, waits for them, and re-layouts  21.6 us (11%)
  matrix products  18.6 us (9%)
  blocking collectives  16.3 us (8%)
    unnamed x4, other arithmetic  30.2 us
    ppermute x4, waiting for transfers between devices, with_halo(): lax.ppermute(lax.slice_in_dim(block, 0, width, axis=dim), axis, backward)  28.7 us
    ppermute x4, starting transfers between devices, with_halo(): lax.ppermute(lax.slice_in_dim(block, block.shape[dim] - width, None, axis...  25.8 us
    scatter-add x3, other arithmetic, per_device(): dout_ext.at[source[:, slot]].add(edge_weight[:, slot, None] * dagg)  20.4 us
    ppermute x4, waiting for transfers between devices, with_halo(): lax.ppermute(lax.slice_in_dim(block, block.shape[dim] - width, None, axis...  18.3 us
    all_gather x1, blocking collectives, per_device(): lax.all_gather(prediction[None], 'member', axis=0, tiled=True)  16.3 us
    ppermute x4, starting transfers between devices, with_halo(): lax.ppermute(lax.slice_in_dim(block, 0, width, axis=dim), axis, backward)  13.9 us
    gather x3, local copies, waits for them, and re-layouts, per_device(): output_ext[source[:, slot]].astype(jnp.float32)  7.64 us
  transfers between devices with their start and end apart: 8, of which 6 were waited for; matrix products, arithmetic and copies ran while one was open for 17% of the time, Pallas kernels for 0%

commit v1 on v0

v1 whole, which is shorter than its diff:
```python
import jax
import jax.numpy as jnp
from jax import lax
from jax.experimental import pallas as pl
from jax.experimental.pallas import tpu as pltpu
from jax.sharding import PartitionSpec as P

HEADS = 8
DH = 64
PAIRS = HEADS // 2
KW = 32
KD = 3
V = 100
VP = 128
EDGE = 64
OWN = 128
D = 1024
E = HEADS * DH
G = 512
MEMBERS = 8
SHARDS = 64

score_scale = 6.0
eps_norm = 1e-06
delta_smooth = 0.1

MESH = pl.DeviceIdType.MESH
f32 = jnp.float32
bf16 = jnp.bfloat16


def dot(a, b):
    return jnp.dot(a, b, preferred_element_type=f32)


def dot_t(a, b):
    return lax.dot_general(a, b, (((1,), (1,)), ((), ())), preferred_element_type=f32)


def smooth_slope(difference):
    return difference * lax.rsqrt(difference * difference + delta_smooth * delta_smooth)


def head_ones():
    row = lax.broadcasted_iota(jnp.int32, (128, 128), 0) < DH
    lane = lax.broadcasted_iota(jnp.int32, (128, 128), 1) < DH
    return jnp.where(row == lane, 1.0, 0.0).astype(bf16)


def head_means(values, ones):
    low = values.astype(bf16)
    parts = [dot(low[:, 128 * p : 128 * (p + 1)], ones) for p in range(PAIRS)]
    return jnp.concatenate(parts, axis=1) * (1.0 / DH)


def normalize(projected, ones):
    factor = lax.rsqrt(head_means(projected * projected, ones) + eps_norm)
    return projected * factor, factor


def norm_backward(grad_hat, unit_rows, factor, ones):
    return factor * (grad_hat - unit_rows * head_means(grad_hat * unit_rows, ones))


def kernel(
    latent, w_query, w_key, w_value, w_out, w_decode, window, source, edge_weight, target, area,
    out,
    x, xh, wq, wk, wv, wo, wd_raw, wd, win, src, ew, tgt, area_row,
    q_hat, q_factor, k_hat, k_factor, q_low, key_pair, value_pair,
    weight, weight_t, counts2, counts_t, count_send, count_recv, numden, mixed, mixed_halo, inverse,
    pred_rows, spread, gather, truth, fold, base, sums, sums_low, from_left, from_right,
    local_sem, halo_send, halo_recv, member_send, member_recv,
):
    m = lax.axis_index("member")
    s = lax.axis_index("space")
    has_left = s > 0
    has_right = s < SHARDS - 1
    left = (m, lax.rem(s + SHARDS - 1, SHARDS))
    right = (m, lax.rem(s + 1, SHARDS))
    peers = [(lax.rem(m + d, MEMBERS), s) for d in range(MEMBERS)]

    barrier = pltpu.get_barrier_semaphore()

    @pl.when(has_left)
    def _():
        pl.semaphore_signal(barrier, inc=1, device_id=left, device_id_type=MESH)

    @pl.when(has_right)
    def _():
        pl.semaphore_signal(barrier, inc=1, device_id=right, device_id_type=MESH)

    for d in range(1, MEMBERS):
        pl.semaphore_signal(barrier, inc=1, device_id=peers[d], device_id_type=MESH)

    pairs = [
        (latent.at[0], x), (window, win), (w_decode, wd_raw), (w_key, wk), (w_value, wv),
        (w_query, wq), (w_out, wo), (source, src), (edge_weight, ew), (target, tgt),
        (area, area_row),
    ]
    loads = [pltpu.make_async_copy(a, b, local_sem.at[i]) for i, (a, b) in enumerate(pairs)]
    for load in loads:
        load.start()
    (x_load, win_load, wd_load, wk_load, wv_load, wq_load, wo_load, src_load, ew_load, tgt_load,
     area_load) = loads

    @pl.when(jnp.logical_not(has_left))
    def _():
        xh[EDGE:] = jnp.zeros((EDGE, D), bf16)
        count_recv[:EDGE] = jnp.zeros((EDGE, OWN), bf16)
        pred_rows[OWN + EDGE :, :VP] = jnp.zeros((EDGE, VP), bf16)
        mixed_halo[EDGE:] = jnp.zeros((EDGE, E + 128), bf16)
        from_left[...] = jnp.zeros((2 * EDGE, VP), bf16)

    @pl.when(jnp.logical_not(has_right))
    def _():
        xh[:EDGE] = jnp.zeros((EDGE, D), bf16)
        count_recv[EDGE:] = jnp.zeros((EDGE, OWN), bf16)
        pred_rows[OWN : OWN + EDGE, :VP] = jnp.zeros((EDGE, VP), bf16)
        mixed_halo[:EDGE] = jnp.zeros((EDGE, E + 128), bf16)
        from_right[...] = jnp.zeros((2 * EDGE, VP), bf16)

    def halo(index, to_left, to_right):
        copies = [
            pltpu.make_async_remote_copy(
                src_ref=a, dst_ref=b, send_sem=halo_send.at[index, side],
                recv_sem=halo_recv.at[index, side], device_id=device, device_id_type=MESH,
            )
            for side, (a, b), device in ((0, to_left, left), (1, to_right, right))
        ]

        def start():
            @pl.when(has_left)
            def _():
                copies[0].start()

            @pl.when(has_right)
            def _():
                copies[1].start()

        def arrive():
            @pl.when(has_right)
            def _():
                copies[0].wait_recv()

            @pl.when(has_left)
            def _():
                copies[1].wait_recv()

        def leave():
            @pl.when(has_left)
            def _():
                copies[0].wait_send()

            @pl.when(has_right)
            def _():
                copies[1].wait_send()

        return start, arrive, leave

    def member_copies(index, rows):
        return [
            pltpu.make_async_remote_copy(
                src_ref=pred_rows.at[rows, pl.ds(0, VP)],
                dst_ref=pred_rows.at[rows, pl.ds(VP * d, VP)],
                send_sem=member_send.at[index, d],
                recv_sem=member_recv.at[index, d],
                device_id=peers[d],
                device_id_type=MESH,
            )
            for d in range(1, MEMBERS)
        ]

    lower, upper = pl.ds(0, EDGE), pl.ds(EDGE, EDGE)
    latent_halo = halo(0, (x.at[lower], xh.at[lower]), (x.at[upper], xh.at[upper]))
    count_halo = halo(
        1, (count_send.at[upper], count_recv.at[upper]), (count_send.at[lower], count_recv.at[lower])
    )
    pred_halo = halo(
        2,
        (pred_rows.at[lower, pl.ds(0, VP)], pred_rows.at[pl.ds(OWN, EDGE), pl.ds(0, VP)]),
        (pred_rows.at[upper, pl.ds(0, VP)], pred_rows.at[pl.ds(OWN + EDGE, EDGE), pl.ds(0, VP)]),
    )
    mixed_exchange = halo(
        3, (mixed.at[lower], mixed_halo.at[lower]), (mixed.at[upper], mixed_halo.at[upper])
    )
    sum_exchange = halo(
        4,
        (sums_low.at[pl.ds(OWN + EDGE, 2 * EDGE)], from_right),
        (sums_low.at[pl.ds(EDGE, 2 * EDGE)], from_left),
    )

    x_load.wait()
    one = jnp.int32(1)
    pl.semaphore_wait(
        barrier, MEMBERS - 1 + jnp.minimum(s, one) + jnp.minimum(SHARDS - 1 - s, one)
    )

    latent_halo[0]()

    ones = head_ones()
    lane = lax.broadcasted_iota(jnp.int32, (128, 128), 1)
    first_head = lane < DH
    first_ones = jnp.where(first_head, 1.0, 0.0).astype(bf16)
    second_ones = jnp.where(first_head, 0.0, 1.0).astype(bf16)

    win_load.wait()
    near = jnp.bitwise_and(win[...] - s * OWN, 255)
    place = lax.broadcasted_iota(jnp.int32, (256, 128), 0)
    turned = jnp.zeros((256, OWN), f32)
    for k in range(KW):
        turned = turned + jnp.where(near[k : k + 1] == place, 1.0, 0.0)
    counts = turned.T
    count_send[...] = turned[OWN:].astype(bf16)
    count_halo[0]()
    own_counts, halo_counts = counts[:, :OWN], counts[:, OWN:]
    counts2[...] = jnp.concatenate([own_counts, own_counts, halo_counts, halo_counts], axis=1)
    counts_t[...] = turned[:OWN]

    def split_pair(values):
        return jnp.concatenate(
            [jnp.where(first_head, values, 0.0), jnp.where(first_head, 0.0, values)], axis=0
        ).astype(bf16)

    def put_keys(rows, where, keep):
        k_unit, k_scale = normalize(dot(rows, wk[...]), ones)
        values = dot(rows, wv[...])
        if keep:
            k_hat[...] = k_unit
            k_factor[...] = k_scale
        for p in range(PAIRS):
            cols = slice(128 * p, 128 * (p + 1))
            key_pair[p, where : where + 256] = split_pair(k_unit[:, cols])
            value_pair[p, where : where + 256, :128] = split_pair(values[:, cols])
            value_pair[p, where : where + 128, 128:] = first_ones
            value_pair[p, where + 128 : where + 256, 128:] = second_ones

    def put_queries(rows, where, keep):
        q_unit, q_scale = normalize(dot(rows, wq[...]), ones)
        if keep:
            q_hat[...] = q_unit
            q_factor[...] = q_scale
        q_low[where : where + OWN] = (q_unit * (score_scale / DH)).astype(bf16)

    own_rows = x[...]
    wk_load.wait()
    wv_load.wait()
    put_keys(own_rows, 0, True)
    wq_load.wait()
    put_queries(own_rows, 0, True)

    def attend(p, where):
        cols = slice(128 * p, 128 * (p + 1))
        scores = dot_t(q_low[:OWN, cols], key_pair[p, where : where + 256])
        chosen = (counts2[:, where : where + 256] * jnp.exp(scores)).astype(bf16)
        weight[p, :, where : where + 256] = chosen
        return dot(chosen, value_pair[p, where : where + 256])

    def attend_turned(p, where, count_turned):
        cols = slice(128 * p, 128 * (p + 1))
        scores = dot_t(key_pair[p, :256], q_low[where : where + OWN, cols])
        twice = jnp.concatenate([count_turned, count_turned], axis=0)
        weight_t[p, :, where : where + OWN] = (twice * jnp.exp(scores)).astype(bf16)

    for p in range(PAIRS):
        numden[p] = attend(p, 0)

    wd_load.wait()
    wd[...] = jnp.zeros((VP, D), bf16)
    wd[:V] = wd_raw[...]
    base[...] = dot_t(own_rows, wd[...])
    wo_load.wait()
    fold[...] = dot_t(wd[...], wo[...]).astype(bf16)

    src_load.wait()
    ew_load.wait()
    area_load.wait()
    tgt_load.wait()
    for g in range(0, G, 128):
        near = jnp.bitwise_and(src[:, g : g + 128] - s * OWN, 255)
        edges = jnp.zeros((256, 128), f32)
        for k in range(KD):
            edges = edges + jnp.where(near[k : k + 1] == place, ew[k : k + 1, g : g + 128], 0.0)
        gather[g : g + 128] = edges.T.astype(bf16)
        spread[:, g : g + 128] = (edges * area_row[:, g : g + 128]).astype(bf16)
        block = tgt[:, g : g + 128].astype(f32)
        truth[g : g + 128] = jnp.concatenate([block, jnp.zeros((VP - V, 128), f32)], axis=0).T

    for p in range(PAIRS):
        attend_turned(p, 0, counts_t[...])

    latent_halo[1]()
    halo_rows = xh[...]
    put_keys(halo_rows, 256, False)
    compact = jnp.zeros((OWN, 128), f32)
    for p in range(PAIRS):
        cols = slice(128 * p, 128 * (p + 1))
        both = numden[p] + attend(p, 256)
        recip = 1.0 / both[:, 128:]
        inverse[:, cols] = recip
        mixed[:, cols] = (both[:, :128] * recip).astype(bf16)
        compact = jnp.where(jnp.bitwise_and(lane, DH - 1) == p, recip, compact)
    mixed[:, E:] = compact.astype(bf16)
    pred_rows[:OWN, :VP] = (base[...] + dot_t(mixed[:, :E], fold[...])).astype(bf16)
    pred_halo[0]()
    own_out = member_copies(0, pl.ds(0, OWN))
    for copy in own_out:
        copy.start()
    mixed_exchange[0]()

    put_queries(halo_rows, OWN, False)
    count_halo[1]()
    for p in range(PAIRS):
        attend_turned(p, OWN, count_recv[...].astype(f32))

    pred_halo[1]()
    halo_out = member_copies(1, pl.ds(OWN, OWN))
    for copy in halo_out:
        copy.start()
    for copy in own_out:
        copy.wait_recv()
    for copy in halo_out:
        copy.wait_recv()

    total = jnp.zeros((256, VP), f32)
    for g in range(0, G, 128):
        rows = gather[g : g + 128]
        mine = dot(rows, pred_rows[:, :VP])
        slopes = jnp.zeros((128, VP), f32)
        for d in range(1, MEMBERS):
            slopes = slopes + smooth_slope(mine - dot(rows, pred_rows[:, VP * d : VP * (d + 1)]))
        dpred = smooth_slope(mine - truth[g : g + 128]) - slopes * (1.0 / (MEMBERS - 1))
        total = total + dot(spread[:, g : g + 128], dpred.astype(bf16))
    sums[...] = total
    sums_low[:256] = total.astype(bf16)
    sums_low[256:] = total[:EDGE].astype(bf16)
    sum_exchange[0]()

    mixed_exchange[1]()
    lower_lane = lax.broadcasted_iota(jnp.int32, (128, 128), 0)
    inverse_halo = []
    for p in range(PAIRS):
        pick = jnp.where(lower_lane == jnp.where(first_head, p, p + DH), 1.0, 0.0).astype(bf16)
        inverse_halo.append(dot(mixed_halo[:, E:], pick))

    sum_exchange[1]()
    near_left = from_left[...].astype(f32)
    near_right = from_right[...].astype(f32)
    own_sum = (
        sums[:OWN] + jnp.concatenate([near_left[EDGE:], near_right[:EDGE]], axis=0)
    ).astype(bf16)
    halo_sum = (
        sums[OWN:] + jnp.concatenate([near_right[EDGE:], near_left[:EDGE]], axis=0)
    ).astype(bf16)

    dmixed = dot(own_sum, fold[...]) * inverse[...]
    dmixed_halo = dot(halo_sum, fold[...]) * jnp.concatenate(inverse_halo, axis=1)
    dmixed_all = jnp.concatenate([dmixed, dmixed_halo], axis=0)
    mixed_all = jnp.concatenate([mixed[:, :E], mixed_halo[:, :E]], axis=0).astype(f32)
    dmixed_low = dmixed_all.astype(bf16)
    row_low = (-dmixed_all * mixed_all).astype(bf16)
    dq_parts, dk_parts, dv_parts = [], [], []
    for p in range(PAIRS):
        cols = slice(128 * p, 128 * (p + 1))
        sides = jnp.concatenate([dmixed_low[:, cols], row_low[:, cols]], axis=1)
        dscore = (weight[p].astype(f32) * dot_t(sides[:OWN], value_pair[p])).astype(bf16)
        dq_parts.append(dot(dscore, key_pair[p]) * (score_scale / DH))
        dscore_t = (weight_t[p].astype(f32) * dot_t(value_pair[p, :256], sides)).astype(bf16)
        dk = dot(dscore_t, q_low[:, cols])
        dv = dot(weight_t[p], dmixed_low[:, cols])
        dk_parts.append(jnp.where(first_head, dk[:OWN], dk[OWN:]))
        dv_parts.append(jnp.where(first_head, dv[:OWN], dv[OWN:]))
    dq = norm_backward(jnp.concatenate(dq_parts, axis=1), q_hat[...], q_factor[...], ones)
    dk = norm_backward(jnp.concatenate(dk_parts, axis=1), k_hat[...], k_factor[...], ones)
    dv = jnp.concatenate(dv_parts, axis=1)
    grad = dot(own_sum, wd[...]) + dot_t(dq.astype(bf16), wq[...])
    grad = grad + dot_t(dk.astype(bf16), wk[...])
    grad = grad + dot_t(dv.astype(bf16), wv[...])
    out[0] = grad.astype(bf16)

    for exchange in (latent_halo, count_halo, pred_halo, mixed_exchange, sum_exchange):
        exchange[2]()
    for copy in own_out + halo_out:
        copy.wait_send()


def per_device(
    latent, w_query, w_key, w_value, w_out, w_decode, window, decoder_src, edge_weight, target, area
):
    vmem = pltpu.VMEM
    hbm = pl.BlockSpec(memory_space=pltpu.HBM)
    return pl.pallas_call(
        kernel,
        out_shape=jax.ShapeDtypeStruct((1, OWN, D), bf16),
        in_specs=[hbm] * 11,
        out_specs=pl.BlockSpec(memory_space=pltpu.VMEM),
        scratch_shapes=[
            vmem((OWN, D), bf16),
            vmem((2 * EDGE, D), bf16),
            vmem((D, E), bf16),
            vmem((D, E), bf16),
            vmem((D, E), bf16),
            vmem((E, D), bf16),
            vmem((V, D), bf16),
            vmem((VP, D), bf16),
            vmem((KW, OWN), jnp.int32),
            vmem((KD, G), jnp.int32),
            vmem((KD, G), f32),
            vmem((V, G), bf16),
            vmem((1, G), f32),
            vmem((OWN, E), f32),
            vmem((OWN, E), f32),
            vmem((OWN, E), f32),
            vmem((OWN, E), f32),
            vmem((2 * OWN, E), bf16),
            vmem((PAIRS, 512, 128), bf16),
            vmem((PAIRS, 512, 256), bf16),
            vmem((PAIRS, OWN, 512), bf16),
            vmem((PAIRS, 256, 256), bf16),
            vmem((OWN, 512), f32),
            vmem((OWN, OWN), f32),
            vmem((OWN, OWN), bf16),
            vmem((OWN, OWN), bf16),
            vmem((PAIRS, OWN, 256), f32),
            vmem((OWN, E + 128), bf16),
            vmem((2 * EDGE, E + 128), bf16),
            vmem((OWN, E), f32),
            vmem((256, MEMBERS * VP), bf16),
            vmem((256, G), bf16),
            vmem((G, 256), bf16),
            vmem((G, VP), f32),
            vmem((VP, E), bf16),
            vmem((OWN, VP), f32),
            vmem((256, VP), f32),
            vmem((320, VP), bf16),
            vmem((2 * EDGE, VP), bf16),
            vmem((2 * EDGE, VP), bf16),
            pltpu.SemaphoreType.DMA((11,)),
            pltpu.SemaphoreType.DMA((5, 2)),
            pltpu.SemaphoreType.DMA((5, 2)),
            pltpu.SemaphoreType.DMA((2, MEMBERS)),
            pltpu.SemaphoreType.DMA((2, MEMBERS)),
        ],
        compiler_params=pltpu.CompilerParams(
            collective_id=0, has_side_effects=True, vmem_limit_bytes=40 << 20
        ),
    )(
        latent, w_query, w_key, w_value, w_out, w_decode, window.T, decoder_src.T, edge_weight.T,
        target, area.reshape(1, -1),
    )


def solution(mesh):
    in_specs = (
        P("member", "space", None),
        P(),
        P(),
        P(),
        P(),
        P(),
        P("space", None),
        P("space", None),
        P("space", None),
        P(None, "space"),
        P("space"),
    )
    out_specs = P("member", "space", None)
    return jax.shard_map(
        per_device, mesh=mesh, in_specs=in_specs, out_specs=out_specs, check_vma=False
    )
```

time: 204 us -> 66 us (0.32)
  the two profiles are of different devices: /device:TPU:252 before, /device:TPU:473 now
where the time goes in v1:
time: 66 us; the launch traced here: 65.5 us
  Pallas kernels  54.3 us (82%)
  local copies, waits for them, and re-layouts  11.2 us (17%)
    pallas_call x1, Pallas kernels, per_device(): pl.pallas_call(kernel, out_shape=jax.ShapeDtypeStruct((1, OWN, D), bf16),...  54.3 us
    unnamed x23, local copies, waits for them, and re-layouts  11.2 us

profile of v1, /device:TPU:473, one launch (start us, length us, event | category | flops | bytes accessed | tf_op | source)
XLA Modules:
  0.0 65.5 jit_solution(11320813548045127639)
XLA Ops:
  0.0 0.0 copy-start.10
  0.0 0.7 %copy-done.10 = f32[512]{0:T(512)S(1)} copy-done((f32[512]{0:T(512)S(1)}, f32[512]{0:T(512)}, u32[]{:S(2)}) %copy-start.10) | copy-done | bytes 2072
  0.7 0.0 copy-start
  0.7 1.2 %copy-done = bf16[1024,512]{1,0:T(8,128)(2,1)S(1)} copy-done((bf16[1024,512]{1,0:T(8,128)(2,1)S(1)}, bf16[1024,512]{1,0:T(8,128)(2,1)}, u32[]{:S(2)}) %copy-start) | copy-done | bytes 1048600
  1.9 0.0 copy-start.1
  1.9 1.2 %copy-done.1 = bf16[1024,512]{1,0:T(8,128)(2,1)S(1)} copy-done((bf16[1024,512]{1,0:T(8,128)(2,1)S(1)}, bf16[1024,512]{1,0:T(8,128)(2,1)}, u32[]{:S(2)}) %copy-start.1) | copy-done | bytes 1048600
  3.1 0.0 copy-start.2
  3.1 1.2 %copy-done.2 = bf16[1024,512]{1,0:T(8,128)(2,1)S(1)} copy-done((bf16[1024,512]{1,0:T(8,128)(2,1)S(1)}, bf16[1024,512]{1,0:T(8,128)(2,1)}, u32[]{:S(2)}) %copy-start.2) | copy-done | bytes 1048600
  4.4 0.0 copy-start.3
  4.4 1.2 %copy-done.3 = bf16[512,1024]{1,0:T(8,128)(2,1)S(1)} copy-done((bf16[512,1024]{1,0:T(8,128)(2,1)S(1)}, bf16[512,1024]{1,0:T(8,128)(2,1)}, u32[]{:S(2)}) %copy-start.3) | copy-done | bytes 1048600
  5.6 0.0 copy-start.4
  5.6 0.9 %copy-done.4 = bf16[1,128,1024]{2,1,0:T(8,128)(2,1)S(1)} copy-done((bf16[1,128,1024]{2,1,0:T(8,128)(2,1)S(1)}, bf16[1,128,1024]{2,1,0:T(8,128)(2,1)}, u32[]{:S(2)}) %copy-start.4) | copy-done | bytes 262168
  6.5 0.0 copy-start.5
  6.5 0.9 %copy-done.5 = bf16[100,1024]{1,0:T(8,128)(2,1)S(1)} copy-done((bf16[100,1024]{1,0:T(8,128)(2,1)S(1)}, bf16[100,1024]{1,0:T(8,128)(2,1)}, u32[]{:S(2)}) %copy-start.5) | copy-done | bytes 204824
  7.5 0.0 copy-start.6
  7.5 0.9 %copy-done.6 = bf16[100,512]{1,0:T(8,128)(2,1)S(1)} copy-done((bf16[100,512]{1,0:T(8,128)(2,1)S(1)}, bf16[100,512]{1,0:T(8,128)(2,1)}, u32[]{:S(2)}) %copy-start.6) | copy-done | bytes 102424
  8.4 0.0 copy-start.7
  8.4 0.7 %copy-done.7 = s32[128,32]{0,1:T(8,128)S(1)} copy-done((s32[128,32]{0,1:T(8,128)S(1)}, s32[128,32]{0,1:T(8,128)}, u32[]{:S(2)}) %copy-start.7) | copy-done | bytes 16408
  9.1 0.0 copy-start.8
  9.1 0.7 %copy-done.8 = s32[512,3]{0,1:T(4,128)S(1)} copy-done((s32[512,3]{0,1:T(4,128)S(1)}, s32[512,3]{0,1:T(4,128)}, u32[]{:S(2)}) %copy-start.8) | copy-done | bytes 6168
  9.8 0.0 copy-start.9
  9.8 0.7 %copy-done.9 = f32[512,3]{0,1:T(4,128)S(1)} copy-done((f32[512,3]{0,1:T(4,128)S(1)}, f32[512,3]{0,1:T(4,128)}, u32[]{:S(2)}) %copy-start.9) | copy-done | bytes 6168
  10.5 54.3 %shard_map.109 = bf16[1,128,1024]{2,1,0:T(8,128)(2,1)S(1)} custom-call(bf16[1,128,1024]{2,1,0:T(8,128)(2,1)S(1)} %copy-done.4, bf16[1024,512]{1,0:T(8,128)(2,1)S(1)} %copy-done, bf16[1024,512]{1,0:T(8,128)(2,1)S(1)} %copy-done.1, bf16[1024,512]{1,0:T(8,128)(2,1)S(1)} %copy-done.2, bf16[512,1024]{1,0:T(8,128)(2,1)S(1)} %copy-done.3, ...), custom_call_target="tpu_custom_call" | custom-call | tf_op jit(solution)/shard_map/pallas_call | solution.py:391
  64.8 0.7 %copy.13 = bf16[1,128,1024]{2,1,0:T(8,128)(2,1)} copy(bf16[1,128,1024]{2,1,0:T(8,128)(2,1)S(1)} %shard_map.109) | data formatting | bytes 524288
Async XLA Ops:
  0.0 0.7 %copy-start.10 = (f32[512]{0:T(512)S(1)}, f32[512]{0:T(512)}, u32[]{:S(2)}) copy-start(f32[512]{0:T(512)} %param.21) | copy-start | bytes 6148
  0.7 1.2 %copy-start = (bf16[1024,512]{1,0:T(8,128)(2,1)S(1)}, bf16[1024,512]{1,0:T(8,128)(2,1)}, u32[]{:S(2)}) copy-start(bf16[1024,512]{1,0:T(8,128)(2,1)} %w_query.1) | copy-start | bytes 3145732
  1.9 1.2 %copy-start.1 = (bf16[1024,512]{1,0:T(8,128)(2,1)S(1)}, bf16[1024,512]{1,0:T(8,128)(2,1)}, u32[]{:S(2)}) copy-start(bf16[1024,512]{1,0:T(8,128)(2,1)} %w_key.1) | copy-start | bytes 3145732
  3.1 1.2 %copy-start.2 = (bf16[1024,512]{1,0:T(8,128)(2,1)S(1)}, bf16[1024,512]{1,0:T(8,128)(2,1)}, u32[]{:S(2)}) copy-start(bf16[1024,512]{1,0:T(8,128)(2,1)} %w_value.1) | copy-start | bytes 3145732
  4.4 1.2 %copy-start.3 = (bf16[512,1024]{1,0:T(8,128)(2,1)S(1)}, bf16[512,1024]{1,0:T(8,128)(2,1)}, u32[]{:S(2)}) copy-start(bf16[512,1024]{1,0:T(8,128)(2,1)} %w_out.1) | copy-start | bytes 3145732
  5.6 0.9 %copy-start.4 = (bf16[1,128,1024]{2,1,0:T(8,128)(2,1)S(1)}, bf16[1,128,1024]{2,1,0:T(8,128)(2,1)}, u32[]{:S(2)}) copy-start(bf16[1,128,1024]{2,1,0:T(8,128)(2,1)} %latent.1) | copy-start | bytes 786436
  6.5 0.9 %copy-start.5 = (bf16[100,1024]{1,0:T(8,128)(2,1)S(1)}, bf16[100,1024]{1,0:T(8,128)(2,1)}, u32[]{:S(2)}) copy-start(bf16[100,1024]{1,0:T(8,128)(2,1)} %w_decode.1) | copy-start | bytes 614404
  7.5 0.9 %copy-start.6 = (bf16[100,512]{1,0:T(8,128)(2,1)S(1)}, bf16[100,512]{1,0:T(8,128)(2,1)}, u32[]{:S(2)}) copy-start(bf16[100,512]{1,0:T(8,128)(2,1)} %target.1) | copy-start | bytes 307204
  8.4 0.7 %copy-start.7 = (s32[128,32]{0,1:T(8,128)S(1)}, s32[128,32]{0,1:T(8,128)}, u32[]{:S(2)}) copy-start(s32[128,32]{0,1:T(8,128)} %param.17) | copy-start | bytes 49156
  9.1 0.7 %copy-start.8 = (s32[512,3]{0,1:T(4,128)S(1)}, s32[512,3]{0,1:T(4,128)}, u32[]{:S(2)}) copy-start(s32[512,3]{0,1:T(4,128)} %param.18) | copy-start | bytes 18436
  9.8 0.7 %copy-start.9 = (f32[512,3]{0,1:T(4,128)S(1)}, f32[512,3]{0,1:T(4,128)}, u32[]{:S(2)}) copy-start(f32[512,3]{0,1:T(4,128)} %param.19) | copy-start | bytes 18436

commit v2 on v1

--- a/solution.py
+++ b/solution.py
@@ -441,7 +441,7 @@
             pltpu.SemaphoreType.DMA((2, MEMBERS)),
         ],
         compiler_params=pltpu.CompilerParams(
-            collective_id=0, has_side_effects=True, vmem_limit_bytes=40 << 20
+            collective_id=0, has_side_effects=True, vmem_limit_bytes=60 << 20
         ),
     )(
         latent, w_query, w_key, w_value, w_out, w_decode, window.T, decoder_src.T, edge_weight.T,

time: 66 us -> 56.8 us (0.86)
  local copies, waits for them, and re-layouts: 11.2 us -> 1.67 us
  Pallas kernels: 54.3 us -> 55 us
    unnamed x23 -> x1, local copies, waits for them, and re-layouts: 11.2 us -> 1.67 us
    pallas_call x1, Pallas kernels: 54.3 us -> 55 us  [per_device(): pl.pallas_call(kernel, out_shape=jax.ShapeDtypeStruct((1, OWN, D), bf16),...]
where the time goes in v2:
time: 56.8 us; the launch traced here: 56.6 us
  Pallas kernels  55 us (97%)
  local copies, waits for them, and re-layouts  1.67 us (3%)
    pallas_call x1, Pallas kernels, per_device(): pl.pallas_call(kernel, out_shape=jax.ShapeDtypeStruct((1, OWN, D), bf16),...  55 us
    unnamed x1, local copies, waits for them, and re-layouts  1.67 us

profile of v2, /device:TPU:473, one launch (start us, length us, event | category | flops | bytes accessed | tf_op | source)
XLA Modules:
  0.0 56.6 jit_solution(11864979687990742745)
XLA Ops:
  0.0 55.0 %shard_map.109 = bf16[1,128,1024]{2,1,0:T(8,128)(2,1)} custom-call(bf16[1,128,1024]{2,1,0:T(8,128)(2,1)} %latent.1, bf16[1024,512]{1,0:T(8,128)(2,1)} %w_query.1, bf16[1024,512]{1,0:T(8,128)(2,1)} %w_key.1, bf16[1024,512]{1,0:T(8,128)(2,1)} %w_value.1, bf16[512,1024]{1,0:T(8,128)(2,1)} %w_out.1, bf16[100,1024]{1,0:T(8,128)(2,1)} %w_decode.1, ...), custom_call_target="tpu_custom_call" | custom-call | tf_op jit(solution)/shard_map/pallas_call | solution.py:391
  55.0 1.7 %copy.13 = bf16[1,128,1024]{2,1,0:T(8,128)(2,1)} copy(bf16[1,128,1024]{2,1,0:T(8,128)(2,1)} %shard_map.109) | data formatting | bytes 524288

commit v3 on v2

--- a/solution.py
+++ b/solution.py
@@ -12,6 +12,7 @@
 KD = 3
 V = 100
 VP = 128
+FIRST, SECOND = 112, 120
 EDGE = 64
 OWN = 128
 D = 1024
@@ -67,7 +68,7 @@
     out,
     x, xh, wq, wk, wv, wo, wd_raw, wd, win, src, ew, tgt, area_row,
     q_hat, q_factor, k_hat, k_factor, q_low, key_pair, value_pair,
-    weight, weight_t, counts2, counts_t, count_send, count_recv, numden, mixed, mixed_halo, inverse,
+    weight, weight_t, counts2, counts_t, count_send, count_recv, numden, early, early_halo, mixed, mixed_halo, inverse, inverse_halo, numerator_halo,
     pred_rows, spread, gather, truth, fold, base, sums, sums_low, from_left, from_right,
     local_sem, halo_send, halo_recv, member_send, member_recv,
 ):
@@ -77,7 +78,11 @@
     has_right = s < SHARDS - 1
     left = (m, lax.rem(s + SHARDS - 1, SHARDS))
     right = (m, lax.rem(s + 1, SHARDS))
-    peers = [(lax.rem(m + d, MEMBERS), s) for d in range(MEMBERS)]
+    core = lax.rem(m, 2)
+    peers = [
+        (lax.rem(m - core + d // 2 * 2, MEMBERS) + (core if d % 2 == 0 else 1 - core), s)
+        for d in range(MEMBERS)
+    ]
 
     barrier = pltpu.get_barrier_semaphore()
 
@@ -108,7 +113,7 @@
         xh[EDGE:] = jnp.zeros((EDGE, D), bf16)
         count_recv[:EDGE] = jnp.zeros((EDGE, OWN), bf16)
         pred_rows[OWN + EDGE :, :VP] = jnp.zeros((EDGE, VP), bf16)
-        mixed_halo[EDGE:] = jnp.zeros((EDGE, E + 128), bf16)
+        early_halo[EDGE:] = jnp.zeros((EDGE, E), bf16)
         from_left[...] = jnp.zeros((2 * EDGE, VP), bf16)
 
     @pl.when(jnp.logical_not(has_right))
@@ -116,7 +121,7 @@
         xh[:EDGE] = jnp.zeros((EDGE, D), bf16)
         count_recv[EDGE:] = jnp.zeros((EDGE, OWN), bf16)
         pred_rows[OWN : OWN + EDGE, :VP] = jnp.zeros((EDGE, VP), bf16)
-        mixed_halo[:EDGE] = jnp.zeros((EDGE, E + 128), bf16)
+        early_halo[:EDGE] = jnp.zeros((EDGE, E), bf16)
         from_right[...] = jnp.zeros((2 * EDGE, VP), bf16)
 
     def halo(index, to_left, to_right):
@@ -157,7 +162,20 @@
 
         return start, arrive, leave
 
-    def member_copies(index, rows):
+    def relay_copies(index, rows):
+        return [
+            pltpu.make_async_remote_copy(
+                src_ref=pred_rows.at[rows, pl.ds(VP * d, VP)],
+                dst_ref=pred_rows.at[rows, pl.ds(VP * (d + 1), VP)],
+                send_sem=member_send.at[index, d + 1],
+                recv_sem=member_recv.at[index, d + 1],
+                device_id=peers[1],
+                device_id_type=MESH,
+            )
+            for d in (2, 4, 6)
+        ]
+
+    def member_copies(index, rows, slots=range(1, MEMBERS)):
         return [
             pltpu.make_async_remote_copy(
                 src_ref=pred_rows.at[rows, pl.ds(0, VP)],
@@ -167,7 +185,7 @@
                 device_id=peers[d],
                 device_id_type=MESH,
             )
-            for d in range(1, MEMBERS)
+            for d in slots
         ]
 
     lower, upper = pl.ds(0, EDGE), pl.ds(EDGE, EDGE)
@@ -180,8 +198,8 @@
         (pred_rows.at[lower, pl.ds(0, VP)], pred_rows.at[pl.ds(OWN, EDGE), pl.ds(0, VP)]),
         (pred_rows.at[upper, pl.ds(0, VP)], pred_rows.at[pl.ds(OWN + EDGE, EDGE), pl.ds(0, VP)]),
     )
-    mixed_exchange = halo(
-        3, (mixed.at[lower], mixed_halo.at[lower]), (mixed.at[upper], mixed_halo.at[upper])
+    early_exchange = halo(
+        3, (early.at[lower], early_halo.at[lower]), (early.at[upper], early_halo.at[upper])
     )
     sum_exchange = halo(
         4,
@@ -262,7 +280,9 @@
         weight_t[p, :, where : where + OWN] = (twice * jnp.exp(scores)).astype(bf16)
 
     for p in range(PAIRS):
-        numden[p] = attend(p, 0)
+        both = attend(p, 0)
+        numden[p] = both
+        early[:, 128 * p : 128 * (p + 1)] = both[:, :128].astype(bf16)
 
     wd_load.wait()
     wd[...] = jnp.zeros((VP, D), bf16)
@@ -288,35 +308,58 @@
     for p in range(PAIRS):
         attend_turned(p, 0, counts_t[...])
 
+    latent_halo[2]()
+    early_exchange[0]()
+
     latent_halo[1]()
     halo_rows = xh[...]
     put_keys(halo_rows, 256, False)
-    compact = jnp.zeros((OWN, 128), f32)
+    decoded = base[...]
     for p in range(PAIRS):
         cols = slice(128 * p, 128 * (p + 1))
         both = numden[p] + attend(p, 256)
         recip = 1.0 / both[:, 128:]
         inverse[:, cols] = recip
         mixed[:, cols] = (both[:, :128] * recip).astype(bf16)
-        compact = jnp.where(jnp.bitwise_and(lane, DH - 1) == p, recip, compact)
-    mixed[:, E:] = compact.astype(bf16)
-    pred_rows[:OWN, :VP] = (base[...] + dot_t(mixed[:, :E], fold[...])).astype(bf16)
+        decoded = jnp.where(lane == SECOND + p, recip, decoded)
+        decoded = jnp.where(lane == FIRST + p, pltpu.roll(recip, DH, 1), decoded)
+    pred_rows[:OWN, :VP] = (decoded + dot_t(mixed[...], fold[...])).astype(bf16)
     pred_halo[0]()
-    own_out = member_copies(0, pl.ds(0, OWN))
+    own_out = member_copies(0, pl.ds(0, OWN), (4, 2, 6, 1))
     for copy in own_out:
         copy.start()
-    mixed_exchange[0]()
 
     put_queries(halo_rows, OWN, False)
     count_halo[1]()
-    for p in range(PAIRS):
-        attend_turned(p, OWN, count_recv[...].astype(f32))
+    crossed = count_recv[...].astype(f32)
+    for p in range(PAIRS):
+        attend_turned(p, OWN, crossed)
+    crossed = crossed.T
+    crossed = jnp.concatenate([crossed, crossed], axis=1)
+    for p in range(PAIRS):
+        scores = dot_t(q_low[OWN:, 128 * p : 128 * (p + 1)], key_pair[p, :256])
+        numerator_halo[p] = dot((crossed * jnp.exp(scores)).astype(bf16), value_pair[p, :256, :128])
 
     pred_halo[1]()
     halo_out = member_copies(1, pl.ds(OWN, OWN))
     for copy in halo_out:
         copy.start()
     for copy in own_out:
+        copy.wait_recv()
+    own_relay = relay_copies(0, pl.ds(0, OWN))
+    for copy in own_relay:
+        copy.start()
+    early_exchange[1]()
+    row = lax.broadcasted_iota(jnp.int32, (128, 128), 0)
+    for p in range(PAIRS):
+        cols = slice(128 * p, 128 * (p + 1))
+        pick = jnp.where(row == jnp.where(first_head, FIRST + p, SECOND + p), 1.0, 0.0).astype(bf16)
+        recip = dot(pred_rows[OWN:, :VP], pick)
+        inverse_halo[:, cols] = recip
+        mixed_halo[:, cols] = (
+            (numerator_halo[p] + early_halo[:, cols].astype(f32)) * recip
+        ).astype(bf16)
+    for copy in own_relay:
         copy.wait_recv()
     for copy in halo_out:
         copy.wait_recv()
@@ -335,13 +378,6 @@
     sums_low[256:] = total[:EDGE].astype(bf16)
     sum_exchange[0]()
 
-    mixed_exchange[1]()
-    lower_lane = lax.broadcasted_iota(jnp.int32, (128, 128), 0)
-    inverse_halo = []
-    for p in range(PAIRS):
-        pick = jnp.where(lower_lane == jnp.where(first_head, p, p + DH), 1.0, 0.0).astype(bf16)
-        inverse_halo.append(dot(mixed_halo[:, E:], pick))
-
     sum_exchange[1]()
     near_left = from_left[...].astype(f32)
     near_right = from_right[...].astype(f32)
@@ -353,9 +389,9 @@
     ).astype(bf16)
 
     dmixed = dot(own_sum, fold[...]) * inverse[...]
-    dmixed_halo = dot(halo_sum, fold[...]) * jnp.concatenate(inverse_halo, axis=1)
+    dmixed_halo = dot(halo_sum, fold[...]) * inverse_halo[...]
     dmixed_all = jnp.concatenate([dmixed, dmixed_halo], axis=0)
-    mixed_all = jnp.concatenate([mixed[:, :E], mixed_halo[:, :E]], axis=0).astype(f32)
+    mixed_all = jnp.concatenate([mixed[...], mixed_halo[...]], axis=0).astype(f32)
     dmixed_low = dmixed_all.astype(bf16)
     row_low = (-dmixed_all * mixed_all).astype(bf16)
     dq_parts, dk_parts, dv_parts = [], [], []
@@ -377,9 +413,9 @@
     grad = grad + dot_t(dv.astype(bf16), wv[...])
     out[0] = grad.astype(bf16)
 
-    for exchange in (latent_halo, count_halo, pred_halo, mixed_exchange, sum_exchange):
+    for exchange in (count_halo, pred_halo, early_exchange, sum_exchange):
         exchange[2]()
-    for copy in own_out + halo_out:
+    for copy in own_out + own_relay + halo_out:
         copy.wait_send()
 
 
@@ -421,9 +457,13 @@
             vmem((OWN, OWN), bf16),
             vmem((OWN, OWN), bf16),
             vmem((PAIRS, OWN, 256), f32),
-            vmem((OWN, E + 128), bf16),
-            vmem((2 * EDGE, E + 128), bf16),
+            vmem((OWN, E), bf16),
+            vmem((2 * EDGE, E), bf16),
+            vmem((OWN, E), bf16),
+            vmem((2 * EDGE, E), bf16),
             vmem((OWN, E), f32),
+            vmem((2 * EDGE, E), f32),
+            vmem((PAIRS, 2 * EDGE, 128), f32),
             vmem((256, MEMBERS * VP), bf16),
             vmem((256, G), bf16),
             vmem((G, 256), bf16),

time: 56.8 us -> 53.8 us (0.947)
  the two profiles are of different devices: /device:TPU:473 before, /device:TPU:257 now
where the time goes in v3:
time: 53.8 us; the launch traced here: 53.7 us
  Pallas kernels  52 us (97%)
  local copies, waits for them, and re-layouts  1.67 us (3%)
    pallas_call x1, Pallas kernels, per_device(): pl.pallas_call(kernel, out_shape=jax.ShapeDtypeStruct((1, OWN, D), bf16),...  52 us
    unnamed x1, local copies, waits for them, and re-layouts  1.67 us

profile of v3, /device:TPU:257, one launch (start us, length us, event | category | flops | bytes accessed | tf_op | source)
XLA Modules:
  0.0 53.7 jit_solution(6360338439457584496)
XLA Ops:
  0.0 52.0 %shard_map.109 = bf16[1,128,1024]{2,1,0:T(8,128)(2,1)} custom-call(bf16[1,128,1024]{2,1,0:T(8,128)(2,1)} %latent.1, bf16[1024,512]{1,0:T(8,128)(2,1)} %w_query.1, bf16[1024,512]{1,0:T(8,128)(2,1)} %w_key.1, bf16[1024,512]{1,0:T(8,128)(2,1)} %w_value.1, bf16[512,1024]{1,0:T(8,128)(2,1)} %w_out.1, bf16[100,1024]{1,0:T(8,128)(2,1)} %w_decode.1, ...), custom_call_target="tpu_custom_call" | custom-call | tf_op jit(solution)/shard_map/pallas_call | solution.py:427
  52.0 1.7 %copy.13 = bf16[1,128,1024]{2,1,0:T(8,128)(2,1)} copy(bf16[1,128,1024]{2,1,0:T(8,128)(2,1)} %shard_map.109) | data formatting | bytes 524288

commit v4 on v3

--- a/solution.py
+++ b/solution.py
@@ -76,6 +76,7 @@
     s = lax.axis_index("space")
     has_left = s > 0
     has_right = s < SHARDS - 1
+    even = lax.rem(s, 2) == 0
     left = (m, lax.rem(s + SHARDS - 1, SHARDS))
     right = (m, lax.rem(s + 1, SHARDS))
     core = lax.rem(m, 2)
@@ -133,14 +134,28 @@
             for side, (a, b), device in ((0, to_left, left), (1, to_right, right))
         ]
 
-        def start():
-            @pl.when(has_left)
+        def start(in_turn=False):
+            @pl.when(jnp.logical_and(has_left, even))
             def _():
                 copies[0].start()
+                if in_turn:
+                    copies[0].wait_send()
 
             @pl.when(has_right)
             def _():
                 copies[1].start()
+
+            if in_turn:
+
+                @pl.when(jnp.logical_not(even))
+                def _():
+                    @pl.when(has_right)
+                    def _():
+                        copies[1].wait_send()
+
+            @pl.when(jnp.logical_and(has_left, jnp.logical_not(even)))
+            def _():
+                copies[0].start()
 
         def arrive():
             @pl.when(has_right)
@@ -160,7 +175,16 @@
             def _():
                 copies[1].wait_send()
 
-        return start, arrive, leave
+        def leave_rest():
+            @pl.when(jnp.logical_and(has_left, jnp.logical_not(even)))
+            def _():
+                copies[0].wait_send()
+
+            @pl.when(jnp.logical_and(has_right, even))
+            def _():
+                copies[1].wait_send()
+
+        return start, arrive, leave, leave_rest
 
     def relay_copies(index, rows):
         return [
@@ -213,7 +237,7 @@
         barrier, MEMBERS - 1 + jnp.minimum(s, one) + jnp.minimum(SHARDS - 1 - s, one)
     )
 
-    latent_halo[0]()
+    latent_halo[0](True)
 
     ones = head_ones()
     lane = lax.broadcasted_iota(jnp.int32, (128, 128), 1)
@@ -308,8 +332,7 @@
     for p in range(PAIRS):
         attend_turned(p, 0, counts_t[...])
 
-    latent_halo[2]()
-    early_exchange[0]()
+    latent_halo[3]()
 
     latent_halo[1]()
     halo_rows = xh[...]
@@ -328,6 +351,7 @@
     own_out = member_copies(0, pl.ds(0, OWN), (4, 2, 6, 1))
     for copy in own_out:
         copy.start()
+    early_exchange[0]()
 
     put_queries(halo_rows, OWN, False)
     count_halo[1]()
@@ -341,7 +365,7 @@
         numerator_halo[p] = dot((crossed * jnp.exp(scores)).astype(bf16), value_pair[p, :256, :128])
 
     pred_halo[1]()
-    halo_out = member_copies(1, pl.ds(OWN, OWN))
+    halo_out = member_copies(1, pl.ds(OWN, OWN), (4, 5, 6, 7, 2, 3, 1))
     for copy in halo_out:
         copy.start()
     for copy in own_out:

time: 53.8 us -> 52.1 us (0.968)
  the two profiles are of different devices: /device:TPU:257 before, /device:TPU:200 now
where the time goes in v4:
time: 52.1 us; the launch traced here: 52 us
  Pallas kernels  50.3 us (97%)
  local copies, waits for them, and re-layouts  1.67 us (3%)
    pallas_call x1, Pallas kernels, per_device(): pl.pallas_call(kernel, out_shape=jax.ShapeDtypeStruct((1, OWN, D), bf16),...  50.3 us
    unnamed x1, local copies, waits for them, and re-layouts  1.67 us

profile of v4, /device:TPU:200, one launch (start us, length us, event | category | flops | bytes accessed | tf_op | source)
XLA Modules:
  0.0 52.0 jit_solution(1640888511783660698)
XLA Ops:
  0.0 50.3 %shard_map.109 = bf16[1,128,1024]{2,1,0:T(8,128)(2,1)} custom-call(bf16[1,128,1024]{2,1,0:T(8,128)(2,1)} %latent.1, bf16[1024,512]{1,0:T(8,128)(2,1)} %w_query.1, bf16[1024,512]{1,0:T(8,128)(2,1)} %w_key.1, bf16[1024,512]{1,0:T(8,128)(2,1)} %w_value.1, bf16[512,1024]{1,0:T(8,128)(2,1)} %w_out.1, bf16[100,1024]{1,0:T(8,128)(2,1)} %w_decode.1, ...), custom_call_target="tpu_custom_call" | custom-call | tf_op jit(solution)/shard_map/pallas_call | solution.py:451
  50.3 1.7 %copy.13 = bf16[1,128,1024]{2,1,0:T(8,128)(2,1)} copy(bf16[1,128,1024]{2,1,0:T(8,128)(2,1)} %shard_map.109) | data formatting | bytes 524288
